TPU v7x, 32 devices: a whole 2x2x4 slice. The times are simulated.
32 devices in a mesh: prow: 8 (over z, x), pcol: 4 (over y, core).
Axes of the slice: x: 2, y: 2, z: 4, core: 2. Of those that a mesh axis runs over, the one named last changes fastest.
Arguments:
- pool_inverse: float32 [2048, 2048], P('prow', 'pcol'), may hold values from -6 to 6
- panel_blocks: float32 [1, 2048, 512], P(None, 'prow'), may hold values from -0.1875 to 0.1875
- prev_panel: float32 [1, 512, 512], P(None, 'prow'), may hold values from -0.25 to 0.25
- pivot_inverse: float32 [1, 512, 512], P(None, 'pcol'), may hold values from -6 to 6
- top_column: float32 [512, 2048], P('pcol', 'prow'), may hold values from -6 to 6
- top_diag: float32 [512, 512], P('pcol'), may hold values from -6 to 6
- slot_blocks: int32 [1, 16], replicated, may hold values from -1 to 15, as said below
Outputs:
- column_out: float32 [1, 512, 2048], P(None, 'pcol', 'prow')
- cross_out: float32 [1, 512, 512], P(None, 'pcol')
- diag_out: float32 [1, 512, 512], P(None, 'pcol')
Inputs may be any that keep to these rules, and one draw needn't show every extreme that they name: `slot_blocks`: row owner r's slots, entries r * 2 to r * 2 + 1 of a supernode's list, name distinct pool blocks of r * 2 to r * 2 + 1 in ascending order, followed by -1 for unused slots. In every supernode the 2 row owners of some aligned group of 2 use all their slots.
All inputs are finite; a program needn't handle non-finite values.
Results may differ from a plain program's by a relative error of at most 0.0001.
Values sent between devices are 32-bit elements; how exact they have to be, the bound alone decides.
A program may use at most 64 MiB of HBM per device.

v0:
```python
import jax
import jax.numpy as jnp
from jax import lax
from jax.sharding import PartitionSpec as P

BLK = 128
SLOTS = 2


highest = lax.Precision.HIGHEST


def broadcast(value, axis, source):
    kept = jnp.where(lax.axis_index(axis) == source, value, 0).astype(value.dtype)
    return lax.psum(kept, axis)


def matmul(left, right):
    return jnp.dot(left, right, precision=highest, preferred_element_type=jnp.float32)


def contract_first(left, right):
    return lax.dot_general(
        left, right, (((0,), (0,)), ((), ())), precision=highest, preferred_element_type=jnp.float32
    )


def body(pool_inverse, panel_blocks, prev_panel, pivot_inverse, top_column, top_diag, slot_blocks):
    row_rank = lax.axis_index("prow")
    col_rank = lax.axis_index("pcol")
    groups = lax.axis_size("prow") // lax.axis_size("pcol")
    row_count = pool_inverse.shape[0]
    col_blocks = pool_inverse.shape[1] // BLK
    row_blocks = row_count // BLK
    col_width = pivot_inverse.shape[1]
    thin_rows = prev_panel.shape[1]

    def own_slots(supernode):
        return lax.dynamic_slice_in_dim(slot_blocks[supernode], row_rank * SLOTS, SLOTS)

    def own_panel(supernode):
        keep_rows = jnp.repeat((own_slots(supernode) >= 0).astype(jnp.float32), BLK)
        return panel_blocks[supernode] * keep_rows[:, None]

    diag_rows = top_diag
    supernode = 0
    source = (own_panel(supernode), prev_panel[supernode])
    panels = []
    factors = []
    for member in range(groups):
        received = (
            broadcast(source[0], "prow", groups * col_rank + member),
            broadcast(source[1], "prow", groups * col_rank + member),
        )
        panels.append(received[0])
        factors.append(received[1])
    col_panel = jnp.concatenate(panels, 0)
    col_factor = jnp.concatenate(factors, 0)
    column_ids = lax.dynamic_slice_in_dim(
        slot_blocks[supernode], groups * col_rank * SLOTS, groups * SLOTS
    )
    column_local = jnp.clip(column_ids - col_rank * col_blocks, 0, col_blocks - 1)
    picked = jnp.take(
        pool_inverse.reshape(row_count, col_blocks, BLK), column_local, axis=1
    ).reshape(row_count, -1)
    first_part = lax.dot_general(
        col_panel,
        picked,
        (((0,), (1,)), ((), ())),
        precision=highest,
        preferred_element_type=jnp.float32,
    )
    fresh_column = -lax.psum_scatter(
        first_part + contract_first(col_factor, top_column), "pcol", scatter_dimension=0, tiled=True
    )
    panel_own = own_panel(supernode)
    factor_own = prev_panel[supernode]
    row_local = jnp.clip(own_slots(supernode) - row_rank * row_blocks, 0, row_blocks - 1)

    def pick_rows(source_field):
        return jnp.take(
            source_field.reshape(col_width, row_blocks, BLK), row_local, axis=1
        ).reshape(col_width, -1)

    diag_slice = lax.dynamic_slice_in_dim(diag_rows, row_rank * thin_rows, thin_rows, 1)
    cross_term = matmul(pick_rows(top_column), panel_own) + matmul(diag_slice, factor_own)
    cross_rows = -lax.psum(cross_term, "prow")
    turned = lax.all_to_all(cross_rows, "pcol", split_axis=1, concat_axis=0, tiled=True)
    cross_piece = lax.dynamic_slice_in_dim(turned, row_rank * thin_rows, thin_rows, 0)
    diag_term = matmul(pick_rows(fresh_column), panel_own) + contract_first(cross_piece, factor_own)
    new_diag = pivot_inverse[supernode] - lax.psum(diag_term, "prow")
    cross_rows, diag_rows = (cross_rows, new_diag)
    columns_out = [fresh_column]
    cross_out = [cross_rows]
    diag_out = [diag_rows]
    return (jnp.stack(columns_out), jnp.stack(cross_out), jnp.stack(diag_out))


def solution(mesh):
    in_specs = (
        P("prow", "pcol"),
        P(None, "prow", None),
        P(None, "prow", None),
        P(None, "pcol", None),
        P("pcol", "prow"),
        P("pcol", None),
        P(),
    )
    out_specs = (P(None, "pcol", "prow"), P(None, "pcol", None), P(None, "pcol", None))
    return jax.shard_map(body, mesh=mesh, in_specs=in_specs, out_specs=out_specs, check_vma=False)
```

profile of v0, /device:TPU:0, one launch (start us, length us, event | category | flops | bytes accessed | tf_op | source)
XLA Modules:
  0.0 216.7 jit_solution(6011141357287063043)
XLA Ops:
  7.2 0.7 copy-done.8
  8.1 1.0 copy.15
  9.2 0.6 gather_fusion.1
  10.1 0.5 fusion.5
  10.7 1.1 fusion.8
  11.8 0.7 bitcast_select_fusion.2
  12.5 1.1 convolution_add_fusion.2
  13.7 1.0 copy-done.5
  15.2 0.6 gather_fusion
  15.8 0.2 copy.14
  16.2 91.2 %all-reduce.6.cloned.1.call-done = (f32[64,512]{1,0:T(8,128)}, f32[64,512]{1,0:T(8,128)}, f32[256,512]{1,0:T(8,128)}, f32[256,512]{1,0:T(8,128)}, f32[128,512]{1,0:T(8,128)}) async-done(((f32[64,512]{1,0:T(8,128)}, f32[64,512]{1,0:T(8,128)}, f32[256,512]{1,0:T(8,128)}, f32[256,512]{1,0:T(8,128)}, f32[128,512]{1,0:T(8,128)}), (f32[64,512]{1,0:T(8,128)}, f32[64,512]{1,0:T(8,128)}, f32[256,512]{1,0:T(8,128)}, ...) | async-done | bytes 1572880 | tf_op jit(solution)/shard_map/psum | solution.py:15
  107.4 1.6 fusion.11
  109.1 3.7 %convolution_add_fusion = f32[512,256]{1,0:T(8,128)} fusion(f32[512,256]{1,0:T(8,128)S(1)} %fusion.11, f32[256,512]{0,1:T(8,128)S(1)} %bitcast_select_fusion, f32[256,512]{1,0:T(8,128)S(1)} %copy-done.3, f32[256,512]{1,0:T(8,128)} %get-tuple-element.7), kind=kOutput, calls=%fused_computation.3 | convolution fusion | flops 805699584 | bytes 2621440 | tf_op jit(solution)/shard_map/dot_general | solution.py:66
  112.7 0.9 copy-done.7
  113.7 0.7 negate_bitcast_fusion
  114.4 0.7 copy.25
  115.1 3.4 %all-to-all-start = ((f32[128,4,128]{2,0,1:T(8,128)}), f32[128,4,128]{2,0,1:T(8,128)S(1)}, u32[]{:S(2)}, u32[]{:S(2)}) async-start(f32[128,4,128]{2,0,1:T(8,128)} %bitcast.69), calls=%async_computation.1 | async-start | bytes 524288 | tf_op jit(solution)/shard_map/all_to_all | solution.py:88
  118.6 15.0 %reduce-scatter.2.cloned.1.call-done = f32[128,256]{1,0:T(8,128)} async-done(((f32[512,256]{1,0:T(8,128)}), f32[128,256]{1,0:T(8,128)}) %reduce-scatter.2.cloned.1.call-update) | async-done | bytes 131088 | tf_op jit(solution)/shard_map/reduce_scatter | solution.py:73
  133.6 1.6 negate_bitcast_fusion.2
  135.2 0.6 gather_fusion.2
  135.9 0.5 fusion.3
  136.5 1.1 convolution_add_fusion.1
  137.6 70.8 %all-reduce.4.cloned.1.call-done = f32[128,512]{1,0:T(8,128)} async-done(((f32[128,512]{1,0:T(8,128)}), f32[128,512]{1,0:T(8,128)}) %all-reduce.4.cloned.1.call-update) | async-done | bytes 262160 | tf_op jit(solution)/shard_map/psum | solution.py:91
  208.5 1.7 fusion.15
  (39 shorter events, 1.7 us)
Async XLA Ops:
  7.2 5.4 %copy-start = (f32[128,512]{1,0:T(8,128)S(1)}, f32[128,512]{1,0:T(8,128)}, u32[]{:S(2)}) copy-start(f32[128,512]{1,0:T(8,128)} %param.14) | copy-start | bytes 786436
  7.2 100.2 %all-reduce.6.cloned.1.call-start = ((), (), s32[]{:S(2)}) async-start(), calls=%async_computation.4 | async-start | bytes 3145728 | tf_op jit(solution)/shard_map/psum | solution.py:15
  7.2 0.7 copy-start.8
  9.1 1.0 copy-start.1
  10.7 1.1 copy-start.2
  13.6 1.0 copy-start.5
  13.7 119.9 %reduce-scatter.2.cloned.1.call-start = ((), (), s32[]{:S(2)}) async-start(), calls=%async_computation.2 | async-start | bytes 655360 | tf_op jit(solution)/shard_map/reduce_scatter | solution.py:73
  16.1 91.3 %copy-start.4 = (f32[128,256]{1,0:T(8,128)S(1)}, f32[128,256]{1,0:T(8,128)}, u32[]{:S(2)}) copy-start(f32[128,256]{1,0:T(8,128)} %param.13) | copy-start | bytes 393220
  107.4 1.7 copy-start.3
  112.7 0.9 copy-start.7
  115.1 21.3 %all-to-all-start = ((f32[128,4,128]{2,0,1:T(8,128)}), f32[128,4,128]{2,0,1:T(8,128)S(1)}, u32[]{:S(2)}, u32[]{:S(2)}) async-start(f32[128,4,128]{2,0,1:T(8,128)} %bitcast.69), calls=%async_computation.1 | async-start | bytes 524288 | tf_op jit(solution)/shard_map/all_to_all | solution.py:88
  118.5 89.9 %all-reduce.4.cloned.1.call-start = ((), (), s32[]{:S(2)}) async-start(), calls=%async_computation.3 | async-start | bytes 524288 | tf_op jit(solution)/shard_map/psum | solution.py:91
  137.6 70.9 %copy-start.6 = (f32[1,128,512]{2,1,0:T(8,128)S(1)}, f32[1,128,512]{2,1,0:T(8,128)}, u32[]{:S(2)}) copy-start(f32[1,128,512]{2,1,0:T(8,128)} %param.12) | copy-start | bytes 786436
Sparse Core Ops, SparseCore 0:
  13.8 93.5 all-reduce.5
  112.9 20.6 reduce-scatter.1
  137.9 70.5 all-reduce.3
where the time goes:
time: 217 us
  waiting for transfers between devices  177 us (82%)
  between operations  14 us (6%)
  matrix products  8.59 us (4%)
  local copies, waits for them, and re-layouts  7.13 us (3%)
  other arithmetic  6.4 us (3%)
  starting transfers between devices  3.53 us (2%)
    psum x1, waiting for transfers between devices, broadcast(): return lax.psum(kept, axis)  91.2 us
    psum x1, waiting for transfers between devices, body(): new_diag = pivot_inverse[supernode] - lax.psum(diag_term, 'prow')  70.8 us
    reduce_scatter x1, waiting for transfers between devices, body(): lax.psum_scatter(first_part + contract_first(col_factor, top_column), 'pc...  15 us
  transfers between devices with their start and end apart: 4, of which 3 were waited for; matrix products, arithmetic and copies ran while one was open for 3% of the time, Pallas kernels for 0%

commit v1 on v0

v1 whole, which is shorter than its diff:
```python
import functools

import jax
import jax.numpy as jnp
from jax import lax
from jax.experimental import pallas as pl
from jax.experimental.pallas import tpu as pltpu
from jax.sharding import PartitionSpec as P

BLK = 128
MESH = pl.DeviceIdType.MESH
CHUNKS = 4


def mm(left, right, dims=((1,), (0,))):
    return lax.dot_general(
        left, right, (dims, ((), ())), precision=lax.Precision.HIGHEST, preferred_element_type=jnp.float32
    )


def remote(src, dst, send_sem, recv_sem, device):
    return pltpu.make_async_remote_copy(
        src_ref=src, dst_ref=dst, send_sem=send_sem, recv_sem=recv_sem, device_id=device, device_id_type=MESH
    )


def kernel(
    rows, cols,
    slots, pool, panel, prev, pivot, top, diag,
    column_out, cross_out, diag_out,
    fbuf, lz, g, abuf, tbuf, csend, crecv, xbuf, cag, vsend, vrecv, dsend, drecv, dag,
    share_s, share_r, gup_s, gdn_s, gx_s, gz_r, gx_r, cs_s, cs_r, ca_s, ca_r, v_s, v_r, d_s, d_r, da_s, da_r,
):
    r = lax.axis_index("prow")
    c = lax.axis_index("pcol")
    ys = cols // 2
    y, k = c // 2, c % 2
    lines = rows // 2
    h, lo = r // 2, r % 2
    width = top.shape[0]
    thin = prev.shape[0]
    span = pool.shape[0]
    wide = prev.shape[1]
    half = wide // 2
    row_blocks = span // BLK
    n_slots = panel.shape[0] // BLK

    barrier = pltpu.get_barrier_semaphore()

    def greet(row, col):
        pl.semaphore_signal(barrier, inc=1, device_id=(row, col), device_id_type=MESH)

    home = r // 2 == c
    for i in range(1, rows):
        greet((r + i) % rows, c)
        greet((r + i) % rows, r // 2)
    for i in range(1, cols):
        greet(r, (c + i) % cols)
        for m in range(2):
            greet(2 * c + m, (c + i) % cols)

    @pl.when(r // 2 != c)
    def _():
        greet(r, r // 2)

    for m in range(2):
        @pl.when(r != 2 * c + m)
        def _(m=m):
            greet(2 * c + m, c)

    for b in range(row_blocks):
        block = jnp.zeros((BLK, wide), jnp.float32)
        for s in range(n_slots):
            used = jnp.where(slots[0, r * n_slots + s] == r * row_blocks + b, 1.0, 0.0)
            block = block + panel[pl.ds(s * BLK, BLK), :] * used
        fbuf[pl.ds(b * BLK, BLK), :] = block
    lz[...] = jnp.zeros_like(lz)
    lz[pl.ds(pl.multiple_of(r * thin, 8), thin), :] = prev[...]

    def own_columns(value):
        parts = [
            jnp.concatenate([value[:, (2 * q + kk) * width:(2 * q + kk + 1) * width] for q in range(ys)], 1)
            for kk in range(2)
        ]
        return jnp.where(k == 0, parts[0], parts[1])

    @pl.when(h // 2 == y)
    def _():
        mine = 2 * (h - 2 * y) + lo
        g[mine, pl.ds(0, span), :] = own_columns(fbuf[...])
        g[mine, pl.ds(span, thin), :] = own_columns(prev[...])

    abuf[k] = pool[...]
    tbuf[k] = top[...]

    others = 2 * rows + 3 * cols - 2
    pl.semaphore_wait(barrier, jnp.where(home, others - 2, others))

    peer = 1 - k

    step = span // CHUNKS
    pieces = [(i * step, step) for i in range(CHUNKS)] + [(span, thin)]

    def g_ref(b, low, n):
        return g.at[2 * b + low, pl.ds(pieces[n][0], pieces[n][1]), :]

    def up(b, n):
        return remote(g_ref(b, lo, n), g_ref(b, lo, n), gup_s.at[b, n], gz_r.at[b, n], (r + 2, c))

    def down(b, n):
        return remote(g_ref(b, lo, n), g_ref(b, lo, n), gdn_s.at[b, n], gz_r.at[b, n], (r - 2, c))

    def across(b, n):
        return remote(g_ref(b, lo, n), g_ref(b, lo, n), gx_s.at[b, n], gx_r.at[b, n], (r + 1 - 2 * lo, c))

    def forward(b, n):
        s = 2 * y + b

        @pl.when((h >= s) & (h + 1 < lines))
        def _():
            up(b, n).start()

        @pl.when((h <= s) & (h >= 1))
        def _():
            down(b, n).start()

        across(b, n).start()

    order = [len(pieces) - 1] + list(range(CHUNKS))
    for n in order:
        for b in range(2):
            @pl.when(h == 2 * y + b)
            def _(b=b, n=n):
                forward(b, n)

    share = [
        remote(abuf.at[k], abuf.at[k], share_s.at[0], share_r.at[0], (r, 2 * y + peer)),
        remote(tbuf.at[k], tbuf.at[k], share_s.at[1], share_r.at[1], (r, 2 * y + peer)),
    ]
    for copy in share:
        copy.start()

    cross = mm(top[...], fbuf[...]) + mm(diag[...], lz[...])
    for m in range(2):
        for q in range(cols):
            csend[m * cols + q] = cross[m * thin:(m + 1) * thin, q * width:(q + 1) * width]

    def scatter(m, i):
        q = (c + i) % cols
        return remote(csend.at[m * cols + q], crecv.at[r], cs_s.at[m, i], cs_r.at[r], (2 * c + m, q))

    for i in range(1, cols):
        for m in range(2):
            scatter(m, i).start()
    for m in range(2):
        @pl.when(r != 2 * c + m)
        def _(m=m):
            scatter(m, 0).start()

        @pl.when(r == 2 * c + m)
        def _(m=m):
            crecv[r] = csend[m * cols + c]

    for n in order:
        for b in range(2):
            @pl.when(h != 2 * y + b)
            def _(b=b, n=n):
                up(b, n).wait_recv()
                forward(b, n)

    for i in range(1, rows):
        p = (r + i) % rows
        remote(crecv.at[p], crecv.at[p], cs_s.at[0, 0], cs_r.at[p], (p, c)).wait_recv()

    @pl.when(r // 2 != c)
    def _():
        remote(crecv.at[r], crecv.at[r], cs_s.at[0, 0], cs_r.at[r], (r, r // 2)).wait_recv()

    total = crecv[0]
    for p in range(1, rows):
        total = total + crecv[p]
    xbuf[...] = -total
    mine_slot = (r % 2) * cols + c

    def gather_cross(i):
        p = (r + i) % rows
        return remote(xbuf, cag.at[mine_slot], ca_s.at[i], ca_r.at[mine_slot], (p, r // 2))

    for i in range(1, rows):
        gather_cross(i).start()

    @pl.when(r // 2 != c)
    def _():
        gather_cross(0).start()

    @pl.when(r // 2 == c)
    def _():
        cag[mine_slot] = xbuf[...]

    for copy in share:
        copy.wait_recv()
    for n in order:
        for b in range(2):
            low = 1 - lo
            remote(g_ref(b, low, n), g_ref(b, low, n), gx_s.at[b, n], gx_r.at[b, n], (r + 1 - 2 * lo, c)).wait_recv()
    part = jnp.zeros((span, half), jnp.float32)
    for kk in range(2):
        for m in range(2):
            j = 2 * kk + m
            part = part + mm(abuf[kk, :, m * span:(m + 1) * span], g[j, pl.ds(0, span), :])
            part = part + mm(
                tbuf[kk, pl.ds(m * thin, thin), :], g[j, pl.ds(span, thin), :], ((0,), (0,))
            )
    for q in range(ys):
        vsend[q] = part[:, q * width:(q + 1) * width]

    def scatter_v(i):
        q = (y + i) % ys
        return remote(vsend.at[q], vrecv.at[y], v_s.at[i], v_r.at[y], (r, 2 * q + k))

    for i in range(1, ys):
        scatter_v(i).start()
    second = mm(xbuf[...], prev[...], ((0,), (0,)))
    total = vsend[y]
    for i in range(1, ys):
        q = (y + i) % ys
        remote(vrecv.at[q], vrecv.at[q], v_s.at[i], v_r.at[q], (r, 2 * q + k)).wait_recv()
        total = total + vrecv[q]
    column = -total.T
    column_out[...] = column

    term = mm(column, fbuf[...]) + second
    slab = width // rows
    for p in range(rows):
        dsend[p] = term[p * slab:(p + 1) * slab, :]

    def scatter_d(i):
        p = (r + i) % rows
        return remote(dsend.at[p], drecv.at[r], d_s.at[i], d_r.at[r], (p, c))

    for i in range(1, rows):
        scatter_d(i).start()
    total = dsend[r]
    for i in range(1, rows):
        p = (r + i) % rows
        remote(drecv.at[p], drecv.at[p], d_s.at[i], d_r.at[p], (p, c)).wait_recv()
        total = total + drecv[p]
    dag[r] = pivot[r] - total

    def gather_d(i):
        p = (r + i) % rows
        return remote(dag.at[r], dag.at[r], da_s.at[i], da_r.at[r], (p, c))

    for i in range(1, rows):
        gather_d(i).start()

    for i in range(1, cols):
        for m in range(2):
            slot = m * cols + (c + i) % cols
            remote(cag.at[slot], cag.at[slot], ca_s.at[0], ca_r.at[slot], (2 * c + m, (c + i) % cols)).wait_recv()
    for m in range(2):
        @pl.when(r != 2 * c + m)
        def _(m=m):
            slot = m * cols + c
            remote(cag.at[slot], cag.at[slot], ca_s.at[0], ca_r.at[slot], (2 * c + m, c)).wait_recv()
    for m in range(2):
        for q in range(cols):
            cross_out[pl.ds(m * thin, thin), pl.ds(q * width, width)] = cag[m * cols + q]

    for i in range(1, rows):
        p = (r + i) % rows
        remote(dag.at[p], dag.at[p], da_s.at[i], da_r.at[p], (p, c)).wait_recv()
    diag_out[...] = dag[...]

    for copy in share:
        copy.wait_send()
    for n in order:
        for b in range(2):
            s = 2 * y + b

            @pl.when((h >= s) & (h + 1 < lines))
            def _(b=b, n=n):
                up(b, n).wait_send()

            @pl.when((h <= s) & (h >= 1))
            def _(b=b, n=n):
                down(b, n).wait_send()

            across(b, n).wait_send()
    for i in range(1, cols):
        for m in range(2):
            scatter(m, i).wait_send()
    for m in range(2):
        @pl.when(r != 2 * c + m)
        def _(m=m):
            scatter(m, 0).wait_send()
    for i in range(1, rows):
        gather_cross(i).wait_send()

    @pl.when(r // 2 != c)
    def _():
        gather_cross(0).wait_send()

    for i in range(1, ys):
        scatter_v(i).wait_send()
    for i in range(1, rows):
        scatter_d(i).wait_send()
        gather_d(i).wait_send()


def solution(mesh):
    rows, cols = mesh.shape["prow"], mesh.shape["pcol"]
    ys = cols // 2

    def body(pool, panel, prev, pivot, top, diag, slots):
        panel, prev, pivot = panel[0], prev[0], pivot[0]
        span = pool.shape[0]
        width = top.shape[0]
        thin, wide = prev.shape
        half = wide // 2
        slab = width // rows
        f32 = jnp.float32
        vm = pl.BlockSpec(memory_space=pltpu.VMEM)
        dma = pltpu.SemaphoreType.DMA
        n = CHUNKS + 1
        column, cross, new_diag = pl.pallas_call(
            functools.partial(kernel, rows, cols),
            out_shape=(
                jax.ShapeDtypeStruct((width, span), f32),
                jax.ShapeDtypeStruct((width, wide), f32),
                jax.ShapeDtypeStruct((rows, slab, wide), f32),
            ),
            in_specs=[pl.BlockSpec(memory_space=pltpu.SMEM)] + [vm] * 6,
            out_specs=(vm, vm, vm),
            scratch_shapes=[
                pltpu.VMEM((span, wide), f32),
                pltpu.VMEM((wide, wide), f32),
                pltpu.VMEM((4, span + thin, half), f32),
                pltpu.VMEM((2,) + pool.shape, f32),
                pltpu.VMEM((2, width, span), f32),
                pltpu.VMEM((2 * cols, thin, width), f32),
                pltpu.VMEM((rows, thin, width), f32),
                pltpu.VMEM((thin, width), f32),
                pltpu.VMEM((2 * cols, thin, width), f32),
                pltpu.VMEM((ys, span, width), f32),
                pltpu.VMEM((ys, span, width), f32),
                pltpu.VMEM((rows, slab, wide), f32),
                pltpu.VMEM((rows, slab, wide), f32),
                pltpu.VMEM((rows, slab, wide), f32),
                dma((2,)), dma((2,)),
                dma((2, n)), dma((2, n)), dma((2, n)), dma((2, n)), dma((2, n)),
                dma((2, cols)), dma((rows,)), dma((rows,)), dma((2 * cols,)),
                dma((ys,)), dma((ys,)),
                dma((rows,)), dma((rows,)), dma((rows,)), dma((rows,)),
            ],
            compiler_params=pltpu.CompilerParams(
                collective_id=0, has_side_effects=True, vmem_limit_bytes=40 * 2**20
            ),
        )(slots, pool, panel, prev, pivot.reshape(rows, slab, wide), top, diag)
        return column[None], cross[None], new_diag.reshape(1, width, wide)

    in_specs = (
        P("prow", "pcol"),
        P(None, "prow", None),
        P(None, "prow", None),
        P(None, "pcol", None),
        P("pcol", "prow"),
        P("pcol", None),
        P(),
    )
    out_specs = (P(None, "pcol", "prow"), P(None, "pcol", None), P(None, "pcol", None))
    return jax.shard_map(body, mesh=mesh, in_specs=in_specs, out_specs=out_specs, check_vma=False)
```

time: 217 us -> 66.5 us (0.31)
  waiting for transfers between devices: 177 us -> 0 us
  Pallas kernels: 0 us -> 57 us
  between operations: 14 us -> 0.66 us
  matrix products: 8.59 us -> 0 us
  other arithmetic: 6.4 us -> 0 us
  starting transfers between devices: 3.53 us -> 0 us
    psum x2 -> x0, waiting for transfers between devices: 162 us -> none  [the longest x1 91.2 us: broadcast(): return lax.psum(kept, axis)]
    pallas_call x0 -> x1, Pallas kernels: none -> 57 us  [body(): pl.pallas_call(functools.partial(kernel, rows, cols), out_shape=(jax.Shap...]
    reduce_scatter x1 -> x0, waiting for transfers between devices: 15 us -> none  [body(): lax.psum_scatter(first_part + contract_first(col_factor, top_column), 'pc...]
    dot_general x6 -> x0, matrix products: 8.59 us -> none  [the longest x1 3.65 us: body(): lax.dot_general(col_panel, picked, (((0,), (1,)), ((), ())), precision=hi...]
    unnamed x20 -> x17, local copies, waits for them, and re-layouts: 3.89 us -> 8.5 us
    all_to_all x1 -> x0, starting transfers between devices: 3.41 us -> none  [body(): lax.all_to_all(cross_rows, 'pcol', split_axis=1, concat_axis=0, tiled=True)]
    unnamed x2 -> x0, other arithmetic: 2.31 us -> none
  transfers between devices with their start and end apart: 4 -> 0, of which waited for: 3 -> 0; matrix products, arithmetic and copies ran while one was open for 3% -> 0% of each run, Pallas kernels for 0% -> 0%
where the time goes in v1:
time: 66.5 us; the launch traced here: 66.2 us
  Pallas kernels  57 us (86%)
  local copies, waits for them, and re-layouts  8.5 us (13%)
    pallas_call x1, Pallas kernels, body(): pl.pallas_call(functools.partial(kernel, rows, cols), out_shape=(jax.Shap...  57 us
    unnamed x17, local copies, waits for them, and re-layouts  8.5 us

profile of v1, /device:TPU:0, one launch (start us, length us, event | category | flops | bytes accessed | tf_op | source)
XLA Modules:
  0.0 66.2 jit_solution(13370245900590723664)
XLA Ops:
  0.6 0.0 copy-start.6
  0.6 0.6 copy-done.6
  1.3 0.0 copy-start
  1.3 1.0 %copy-done = f32[256,512]{1,0:T(8,128)S(1)} copy-done((f32[256,512]{1,0:T(8,128)S(1)}, f32[256,512]{1,0:T(8,128)}, u32[]{:S(2)}) %copy-start) | copy-done | bytes 524312
  2.3 0.0 copy-start.1
  2.3 1.0 %copy-done.1 = f32[1,256,512]{2,1,0:T(8,128)S(1)} copy-done((f32[1,256,512]{2,1,0:T(8,128)S(1)}, f32[1,256,512]{2,1,0:T(8,128)}, u32[]{:S(2)}) %copy-start.1) | copy-done | bytes 524312
  3.4 0.0 copy-start.2
  3.4 0.9 %copy-done.2 = f32[1,128,512]{2,1,0:T(8,128)S(1)} copy-done((f32[1,128,512]{2,1,0:T(8,128)S(1)}, f32[1,128,512]{2,1,0:T(8,128)}, u32[]{:S(2)}) %copy-start.2) | copy-done | bytes 262168
  4.3 0.0 copy-start.3
  4.3 0.9 %copy-done.3 = f32[128,512]{1,0:T(8,128)S(1)} copy-done((f32[128,512]{1,0:T(8,128)S(1)}, f32[128,512]{1,0:T(8,128)}, u32[]{:S(2)}) %copy-start.3) | copy-done | bytes 262168
  5.3 0.0 copy-start.4
  5.3 0.9 %copy-done.4 = f32[1,64,512]{2,1,0:T(8,128)S(1)} copy-done((f32[1,64,512]{2,1,0:T(8,128)S(1)}, f32[1,64,512]{2,1,0:T(8,128)}, u32[]{:S(2)}) %copy-start.4) | copy-done | bytes 131096
  6.2 0.0 copy-start.5
  6.2 0.9 %copy-done.5 = f32[128,256]{1,0:T(8,128)S(1)} copy-done((f32[128,256]{1,0:T(8,128)S(1)}, f32[128,256]{1,0:T(8,128)}, u32[]{:S(2)}) %copy-start.5) | copy-done | bytes 131096
  7.1 57.0 %shard_map.94 = (f32[128,256]{1,0:T(8,128)S(1)}, f32[128,512]{1,0:T(8,128)S(1)}, f32[8,16,512]{2,1,0:T(8,128)S(1)}) custom-call(s32[1,16]{1,0:T(1,128)S(1)} %copy-done.6, f32[256,512]{1,0:T(8,128)S(1)} %copy-done, f32[256,512]{1,0:T(8,128)S(1)} %bitcast.6, f32[64,512]{1,0:T(8,128)S(1)} %bitcast.11, f32[8,16,512]{2,1,0:T(8,128)S(1)} %bitcast.9, ...), custom_call_target="tpu_custom_call" | custom-call | tf_op jit(solution)/shard_map/pallas_call | solution.py:326
  64.1 0.7 copy.13
  64.8 0.7 %copy.14 = f32[1,128,512]{2,1,0:T(8,128)} copy(f32[1,128,512]{2,1,0:T(8,128)S(1)} %bitcast.8) | data formatting | bytes 524288
  65.5 0.7 %copy.15 = f32[1,128,512]{2,1,0:T(8,128)} copy(f32[1,128,512]{2,1,0:T(8,128)S(1)} %bitcast.7) | data formatting | bytes 524288
Async XLA Ops:
  0.6 0.7 copy-start.6
  1.3 1.0 %copy-start = (f32[256,512]{1,0:T(8,128)S(1)}, f32[256,512]{1,0:T(8,128)}, u32[]{:S(2)}) copy-start(f32[256,512]{1,0:T(8,128)} %pool.1) | copy-start | bytes 1572868
  2.3 1.0 %copy-start.1 = (f32[1,256,512]{2,1,0:T(8,128)S(1)}, f32[1,256,512]{2,1,0:T(8,128)}, u32[]{:S(2)}) copy-start(f32[1,256,512]{2,1,0:T(8,128)} %param.8) | copy-start | bytes 1572868
  3.4 0.9 %copy-start.2 = (f32[1,128,512]{2,1,0:T(8,128)S(1)}, f32[1,128,512]{2,1,0:T(8,128)}, u32[]{:S(2)}) copy-start(f32[1,128,512]{2,1,0:T(8,128)} %param.10) | copy-start | bytes 786436
  4.3 0.9 %copy-start.3 = (f32[128,512]{1,0:T(8,128)S(1)}, f32[128,512]{1,0:T(8,128)}, u32[]{:S(2)}) copy-start(f32[128,512]{1,0:T(8,128)} %diag.1) | copy-start | bytes 786436
  5.3 0.9 %copy-start.4 = (f32[1,64,512]{2,1,0:T(8,128)S(1)}, f32[1,64,512]{2,1,0:T(8,128)}, u32[]{:S(2)}) copy-start(f32[1,64,512]{2,1,0:T(8,128)} %param.9) | copy-start | bytes 393220
  6.2 0.9 %copy-start.5 = (f32[128,256]{1,0:T(8,128)S(1)}, f32[128,256]{1,0:T(8,128)}, u32[]{:S(2)}) copy-start(f32[128,256]{1,0:T(8,128)} %top.1) | copy-start | bytes 393220

commit v2 on v1

--- a/solution.py
+++ b/solution.py
@@ -26,8 +26,9 @@
 
 def kernel(
     rows, cols,
-    slots, pool, panel, prev, pivot, top, diag,
+    slots, pool_in, panel_in, prev_in, pivot_in, top_in, diag_in,
     column_out, cross_out, diag_out,
+    panel, prev, pivot, top, diag, load_s,
     fbuf, lz, g, abuf, tbuf, csend, crecv, xbuf, cag, vsend, vrecv, dsend, drecv, dag,
     share_s, share_r, gup_s, gdn_s, gx_s, gz_r, gx_r, cs_s, cs_r, ca_s, ca_r, v_s, v_r, d_s, d_r, da_s, da_r,
 ):
@@ -37,9 +38,18 @@
     y, k = c // 2, c % 2
     lines = rows // 2
     h, lo = r // 2, r % 2
+    loads = [
+        pltpu.make_async_copy(src, dst, load_s.at[i])
+        for i, (src, dst) in enumerate([
+            (panel_in, panel), (prev_in, prev), (top_in, top), (diag_in, diag),
+            (pivot_in, pivot), (pool_in, abuf.at[k]), (top_in, tbuf.at[k]),
+        ])
+    ]
+    for load in loads:
+        load.start()
     width = top.shape[0]
     thin = prev.shape[0]
-    span = pool.shape[0]
+    span = pool_in.shape[0]
     wide = prev.shape[1]
     half = wide // 2
     row_blocks = span // BLK
@@ -67,6 +77,9 @@
         @pl.when(r != 2 * c + m)
         def _(m=m):
             greet(2 * c + m, c)
+
+    loads[0].wait()
+    loads[1].wait()
 
     for b in range(row_blocks):
         block = jnp.zeros((BLK, wide), jnp.float32)
@@ -90,9 +103,6 @@
         g[mine, pl.ds(0, span), :] = own_columns(fbuf[...])
         g[mine, pl.ds(span, thin), :] = own_columns(prev[...])
 
-    abuf[k] = pool[...]
-    tbuf[k] = top[...]
-
     others = 2 * rows + 3 * cols - 2
     pl.semaphore_wait(barrier, jnp.where(home, others - 2, others))
 
@@ -127,19 +137,23 @@
         across(b, n).start()
 
     order = [len(pieces) - 1] + list(range(CHUNKS))
+    near = jnp.clip(h - 2 * y, 0, 1)
+    far = 1 - near
+    source = h == 2 * y + near
     for n in order:
-        for b in range(2):
-            @pl.when(h == 2 * y + b)
-            def _(b=b, n=n):
-                forward(b, n)
+        @pl.when(source)
+        def _(n=n):
+            forward(near, n)
 
     share = [
-        remote(abuf.at[k], abuf.at[k], share_s.at[0], share_r.at[0], (r, 2 * y + peer)),
-        remote(tbuf.at[k], tbuf.at[k], share_s.at[1], share_r.at[1], (r, 2 * y + peer)),
+        remote(pool_in, abuf.at[k], share_s.at[0], share_r.at[0], (r, 2 * y + peer)),
+        remote(top_in, tbuf.at[k], share_s.at[1], share_r.at[1], (r, 2 * y + peer)),
     ]
     for copy in share:
         copy.start()
 
+    loads[2].wait()
+    loads[3].wait()
     cross = mm(top[...], fbuf[...]) + mm(diag[...], lz[...])
     for m in range(2):
         for q in range(cols):
@@ -161,12 +175,30 @@
         def _(m=m):
             crecv[r] = csend[m * cols + c]
 
+    def product(b, low):
+        j = 2 * b + low
+        left = abuf[b, :, pl.ds(pl.multiple_of(low * span, BLK), span)]
+        out = mm(left, g[j, pl.ds(0, span), :])
+        return out + mm(
+            tbuf[b, pl.ds(pl.multiple_of(low * thin, 8), thin), :], g[j, pl.ds(span, thin), :], ((0,), (0,))
+        )
+
     for n in order:
-        for b in range(2):
-            @pl.when(h != 2 * y + b)
-            def _(b=b, n=n):
-                up(b, n).wait_recv()
-                forward(b, n)
+        @pl.when(jnp.logical_not(source))
+        def _(n=n):
+            up(near, n).wait_recv()
+            forward(near, n)
+
+    part = None
+    for at, n in enumerate(order):
+        up(far, n).wait_recv()
+        forward(far, n)
+        if at == 1:
+            for load in loads[4:]:
+                load.wait()
+            for copy in share:
+                copy.wait_recv()
+            part = product(near, lo)
 
     for i in range(1, rows):
         p = (r + i) % rows
@@ -197,20 +229,12 @@
     def _():
         cag[mine_slot] = xbuf[...]
 
-    for copy in share:
-        copy.wait_recv()
-    for n in order:
-        for b in range(2):
+    part = part + product(far, lo)
+    for b in (near, far):
+        for n in order:
             low = 1 - lo
             remote(g_ref(b, low, n), g_ref(b, low, n), gx_s.at[b, n], gx_r.at[b, n], (r + 1 - 2 * lo, c)).wait_recv()
-    part = jnp.zeros((span, half), jnp.float32)
-    for kk in range(2):
-        for m in range(2):
-            j = 2 * kk + m
-            part = part + mm(abuf[kk, :, m * span:(m + 1) * span], g[j, pl.ds(0, span), :])
-            part = part + mm(
-                tbuf[kk, pl.ds(m * thin, thin), :], g[j, pl.ds(span, thin), :], ((0,), (0,))
-            )
+        part = part + product(b, 1 - lo)
     for q in range(ys):
         vsend[q] = part[:, q * width:(q + 1) * width]
 
@@ -330,9 +354,15 @@
                 jax.ShapeDtypeStruct((width, wide), f32),
                 jax.ShapeDtypeStruct((rows, slab, wide), f32),
             ),
-            in_specs=[pl.BlockSpec(memory_space=pltpu.SMEM)] + [vm] * 6,
+            in_specs=[pl.BlockSpec(memory_space=pltpu.SMEM)] + [pl.BlockSpec(memory_space=pltpu.HBM)] * 6,
             out_specs=(vm, vm, vm),
             scratch_shapes=[
+                pltpu.VMEM(panel.shape, f32),
+                pltpu.VMEM(prev.shape, f32),
+                pltpu.VMEM((rows, slab, wide), f32),
+                pltpu.VMEM(top.shape, f32),
+                pltpu.VMEM(diag.shape, f32),
+                dma((7,)),
                 pltpu.VMEM((span, wide), f32),
                 pltpu.VMEM((wide, wide), f32),
                 pltpu.VMEM((4, span + thin, half), f32),
@@ -354,7 +384,7 @@
                 dma((rows,)), dma((rows,)), dma((rows,)), dma((rows,)),
             ],
             compiler_params=pltpu.CompilerParams(
-                collective_id=0, has_side_effects=True, vmem_limit_bytes=40 * 2**20
+                collective_id=0, has_side_effects=True, vmem_limit_bytes=60 * 2**20
             ),
         )(slots, pool, panel, prev, pivot.reshape(rows, slab, wide), top, diag)
         return column[None], cross[None], new_diag.reshape(1, width, wide)

time: 66.5 us -> 56.3 us (0.85)
  local copies, waits for them, and re-layouts: 8.5 us -> 3.36 us
  Pallas kernels: 57 us -> 52.1 us
    unnamed x17 -> x7, local copies, waits for them, and re-layouts: 8.5 us -> 3.36 us
    pallas_call x1, Pallas kernels: 57 us -> 52.1 us  [body(): pl.pallas_call(functools.partial(kernel, rows, cols), out_shape=(jax.Shap...]
where the time goes in v2:
time: 56.3 us; the launch traced here: 56.1 us
  Pallas kernels  52.1 us (93%)
  local copies, waits for them, and re-layouts  3.36 us (6%)
  between operations  0.65 us (1%)
    pallas_call x1, Pallas kernels, body(): pl.pallas_call(functools.partial(kernel, rows, cols), out_shape=(jax.Shap...  52.1 us
    unnamed x7, local copies, waits for them, and re-layouts  3.36 us

profile of v2, /device:TPU:0, one launch (start us, length us, event | category | flops | bytes accessed | tf_op | source)
XLA Modules:
  0.0 56.1 jit_solution(2683860082869019504)
XLA Ops:
  0.6 52.1 %shard_map.94 = (f32[128,256]{1,0:T(8,128)}, f32[128,512]{1,0:T(8,128)}, f32[8,16,512]{2,1,0:T(8,128)}) custom-call(s32[1,16]{1,0:T(1,128)} %slots.1, f32[256,512]{1,0:T(8,128)} %pool_in.1, f32[256,512]{1,0:T(8,128)} %bitcast.6, f32[64,512]{1,0:T(8,128)} %bitcast.11, f32[8,16,512]{2,1,0:T(8,128)} %bitcast.9, f32[128,256]{1,0:T(8,128)} %top_in.1, ...), custom_call_target="tpu_custom_call" | custom-call | tf_op jit(solution)/shard_map/pallas_call | solution.py:350
  52.8 0.0 copy-start.1
  52.8 1.6 %copy.13 = f32[1,128,256]{2,1,0:T(8,128)} copy(f32[1,128,256]{2,1,0:T(8,128)} %bitcast.10) | data formatting | bytes 262144
  54.4 0.0 copy-done.1
  54.4 0.0 copy-start
  54.4 0.7 %copy.14 = f32[1,128,512]{2,1,0:T(8,128)} copy(f32[1,128,512]{2,1,0:T(8,128)S(1)} %bitcast.8) | data formatting | bytes 524288
  55.1 0.3 copy-done
  55.4 0.7 %copy.15 = f32[1,128,512]{2,1,0:T(8,128)} copy(f32[1,128,512]{2,1,0:T(8,128)S(1)} %bitcast.7) | data formatting | bytes 524288
Async XLA Ops:
  52.8 1.6 %copy-start.1 = (f32[128,512]{1,0:T(8,128)S(1)}, f32[128,512]{1,0:T(8,128)}, u32[]{:S(2)}) copy-start(f32[128,512]{1,0:T(8,128)} %get-tuple-element.7) | copy-start | bytes 786436
  54.4 1.0 %copy-start = (f32[8,16,512]{2,1,0:T(8,128)S(1)}, f32[8,16,512]{2,1,0:T(8,128)}, u32[]{:S(2)}) copy-start(f32[8,16,512]{2,1,0:T(8,128)} %get-tuple-element.8) | copy-start | bytes 786436

commit v3 on v2

--- a/solution.py
+++ b/solution.py
@@ -9,13 +9,21 @@
 
 BLK = 128
 MESH = pl.DeviceIdType.MESH
-CHUNKS = 4
+CHUNKS = 8
+
+
+def halves(value):
+    high = value.astype(jnp.bfloat16)
+    return high, (value - high.astype(jnp.float32)).astype(jnp.bfloat16)
 
 
 def mm(left, right, dims=((1,), (0,))):
-    return lax.dot_general(
-        left, right, (dims, ((), ())), precision=lax.Precision.HIGHEST, preferred_element_type=jnp.float32
-    )
+    def dot(a, b):
+        return lax.dot_general(a, b, (dims, ((), ())), preferred_element_type=jnp.float32)
+
+    left_high, left_low = halves(left)
+    right_high, right_low = halves(right)
+    return dot(left_high, right_high) + (dot(left_high, right_low) + dot(left_low, right_high))
 
 
 def remote(src, dst, send_sem, recv_sem, device):

time: 56.3 us -> 55.2 us (0.980)
  Pallas kernels: 52.1 us -> 51 us
    pallas_call x1, Pallas kernels: 52.1 us -> 51 us  [body(): pl.pallas_call(functools.partial(kernel, rows, cols), out_shape=(jax.Shap...]
where the time goes in v3:
time: 55.2 us; the launch traced here: 55 us
  Pallas kernels  51 us (92%)
  local copies, waits for them, and re-layouts  3.36 us (6%)
  between operations  0.65 us (1%)
    pallas_call x1, Pallas kernels, body(): pl.pallas_call(functools.partial(kernel, rows, cols), out_shape=(jax.Shap...  51 us
    unnamed x7, local copies, waits for them, and re-layouts  3.36 us

profile of v3, /device:TPU:0, one launch (start us, length us, event | category | flops | bytes accessed | tf_op | source)
XLA Modules:
  0.0 55.0 jit_solution(13131335286993853590)
XLA Ops:
  0.6 51.0 %shard_map.94 = (f32[128,256]{1,0:T(8,128)}, f32[128,512]{1,0:T(8,128)}, f32[8,16,512]{2,1,0:T(8,128)}) custom-call(s32[1,16]{1,0:T(1,128)} %slots.1, f32[256,512]{1,0:T(8,128)} %pool_in.1, f32[256,512]{1,0:T(8,128)} %bitcast.6, f32[64,512]{1,0:T(8,128)} %bitcast.11, f32[8,16,512]{2,1,0:T(8,128)} %bitcast.9, f32[128,256]{1,0:T(8,128)} %top_in.1, ...), custom_call_target="tpu_custom_call" | custom-call | tf_op jit(solution)/shard_map/pallas_call | solution.py:358
  51.6 0.0 copy-start.1
  51.6 1.6 %copy.13 = f32[1,128,256]{2,1,0:T(8,128)} copy(f32[1,128,256]{2,1,0:T(8,128)} %bitcast.10) | data formatting | bytes 262144
  53.2 0.0 copy-done.1
  53.2 0.0 copy-start
  53.2 0.7 %copy.14 = f32[1,128,512]{2,1,0:T(8,128)} copy(f32[1,128,512]{2,1,0:T(8,128)S(1)} %bitcast.8) | data formatting | bytes 524288
  53.9 0.3 copy-done
  54.3 0.7 %copy.15 = f32[1,128,512]{2,1,0:T(8,128)} copy(f32[1,128,512]{2,1,0:T(8,128)S(1)} %bitcast.7) | data formatting | bytes 524288
Async XLA Ops:
  51.6 1.6 %copy-start.1 = (f32[128,512]{1,0:T(8,128)S(1)}, f32[128,512]{1,0:T(8,128)}, u32[]{:S(2)}) copy-start(f32[128,512]{1,0:T(8,128)} %get-tuple-element.7) | copy-start | bytes 786436
  53.2 1.0 %copy-start = (f32[8,16,512]{2,1,0:T(8,128)S(1)}, f32[8,16,512]{2,1,0:T(8,128)}, u32[]{:S(2)}) copy-start(f32[8,16,512]{2,1,0:T(8,128)} %get-tuple-element.8) | copy-start | bytes 786436
